TPU v7x, 32 devices: a whole 2x2x4 slice. The times are simulated.
32 devices in a mesh: ctx: 8 (over z, x), dp: 4 (over y, core).
Axes of the slice: x: 2, y: 2, z: 4, core: 2. Of those that a mesh axis runs over, the one named last changes fastest.
Arguments:
- query: bfloat16 [4, 1024, 1024], P('dp', 'ctx'), may hold values from -6 to 6
- key_in: bfloat16 [4, 1024, 1024], P('dp', 'ctx'), may hold values from -6 to 6
- value: bfloat16 [4, 1024, 1024], P('dp', 'ctx'), may hold values from -6 to 6
- cotangent: bfloat16 [4, 1024, 1024], P('dp', 'ctx'), may hold values from -6 to 6
- filters: bfloat16 [32, 1024], P('ctx'), may hold values from -0.1875 to 0.1875
Outputs:
- output: bfloat16 [4, 1024, 1024], P('dp', 'ctx')
- grad_query: bfloat16 [4, 1024, 1024], P('dp', 'ctx')
- grad_key: bfloat16 [4, 1024, 1024], P('dp', 'ctx')
- grad_value: bfloat16 [4, 1024, 1024], P('dp', 'ctx')
- grad_filter: float32 [32, 1024], P('ctx', 'dp')
All inputs are finite; a program needn't handle non-finite values.
Results may differ from a plain program's by a relative error of at most 0.0058.
Values may be sent and summed in bfloat16 or wider, within the bound.
A program may use at most 64 MiB of HBM per device.

v0:
```python
import math

import jax
import jax.numpy as jnp
from jax import lax
from jax.sharding import PartitionSpec as P

CPG = 32
BLK = 256


def group_rows(items):
    count, width, length = items.shape
    groups = width // CPG
    return (
        items.reshape(count, groups, CPG, length)
        .transpose(1, 0, 2, 3)
        .reshape(groups, count * CPG, length)
    )


def ungroup_rows(rows, count):
    groups, columns, length = rows.shape
    return (
        rows.reshape(groups, count, CPG, length)
        .transpose(1, 0, 2, 3)
        .reshape(count, groups * CPG, length)
    )


def band_blocks(filters_local, blocksize):
    groups, length = filters_local.shape
    width = length + blocksize
    extended = jnp.concatenate(
        [filters_local, jnp.zeros((groups, blocksize), filters_local.dtype)], axis=1
    )
    tiled = jnp.tile(extended, (1, blocksize))[:, : blocksize * (width - 1)]
    shifted = tiled.reshape(groups, blocksize, width - 1)[:, :, :length]
    nblocks = length // blocksize
    return shifted.reshape(groups, blocksize, nblocks, blocksize).transpose(0, 2, 1, 3)


def earlier_blocks(rows, blocksize):
    groups, columns, length = rows.shape
    nblocks = length // blocksize
    blocks = rows.reshape(groups, columns, nblocks, blocksize)
    padded = jnp.concatenate(
        [jnp.zeros((groups, columns, nblocks - 1, blocksize), rows.dtype), blocks], axis=2
    )
    return jnp.stack(
        [
            padded[:, :, nblocks - 1 - offset : 2 * nblocks - 1 - offset]
            for offset in range(nblocks)
        ],
        axis=3,
    )


def later_blocks(rows, blocksize):
    groups, columns, length = rows.shape
    nblocks = length // blocksize
    blocks = rows.reshape(groups, columns, nblocks, blocksize)
    padded = jnp.concatenate(
        [blocks, jnp.zeros((groups, columns, nblocks - 1, blocksize), rows.dtype)], axis=2
    )
    return jnp.stack([padded[:, :, offset : offset + nblocks] for offset in range(nblocks)], axis=3)


def convolve(rows, matrices, blocksize):
    earlier = earlier_blocks(rows, blocksize)
    result = jnp.einsum("gridb,gdba->gria", earlier, matrices, preferred_element_type=jnp.float32)
    return result.reshape(rows.shape)


def convolve_adjoint(rows, matrices, blocksize):
    later = later_blocks(rows, blocksize)
    result = jnp.einsum("grjda,gdba->grjb", later, matrices, preferred_element_type=jnp.float32)
    return result.reshape(rows.shape)


def filter_lags(grad_rows, mixed_rows, blocksize):
    groups, columns, length = grad_rows.shape
    nblocks = length // blocksize
    reversed_grads = grad_rows.reshape(groups, columns, nblocks, blocksize)[:, :, :, ::-1]
    earlier = earlier_blocks(mixed_rows, blocksize)
    square = jnp.einsum(
        "gria,gridb->gdab", reversed_grads, earlier, preferred_element_type=jnp.float32
    )
    padded = jnp.concatenate([square, jnp.zeros_like(square)], axis=3)
    padded = padded.reshape(groups, nblocks, 2 * blocksize * blocksize)[
        :, :, : blocksize * (2 * blocksize - 1)
    ]
    diagonal = padded.reshape(groups, nblocks, blocksize, 2 * blocksize - 1).sum(axis=2)
    extended = jnp.concatenate([diagonal, jnp.zeros((groups, nblocks, 1), jnp.float32)], axis=2)
    nearer = extended[:, :, :blocksize][:, :, ::-1]
    farther = extended[:, :, blocksize:][:, :, ::-1]
    farther = jnp.concatenate(
        [farther[:, 1:], jnp.zeros((groups, 1, blocksize), jnp.float32)], axis=1
    )
    return (nearer + farther).reshape(groups, length)


def local(query, key_in, value, cotangent, filters):
    seqcount = query.shape[0]
    mixed = (key_in.astype(jnp.float32) * value.astype(jnp.float32)).astype(jnp.bfloat16)
    gradin = (cotangent.astype(jnp.float32) * query.astype(jnp.float32)).astype(jnp.bfloat16)
    mixed_cols = mixed.transpose(0, 2, 1)
    gradin_cols = gradin.transpose(0, 2, 1)
    matrices = band_blocks(filters, BLK)
    items = lax.all_to_all(mixed_cols, "ctx", split_axis=1, concat_axis=2, tiled=True)
    conv_items = convolve(group_rows(items), matrices, BLK).astype(jnp.bfloat16)
    conv_own = ungroup_rows(conv_items, items.shape[0])
    conv_cols = lax.all_to_all(conv_own, "ctx", split_axis=2, concat_axis=1, tiled=True)
    grad_own = lax.all_to_all(gradin_cols, "ctx", split_axis=1, concat_axis=2, tiled=True)
    grad_rows = group_rows(grad_own)
    adjoint_own = ungroup_rows(
        convolve_adjoint(grad_rows, matrices, BLK).astype(jnp.bfloat16), seqcount
    )
    adjoint_cols = lax.all_to_all(adjoint_own, "ctx", split_axis=2, concat_axis=1, tiled=True)
    lag_sums = filter_lags(grad_rows, group_rows(items), BLK)
    conv = conv_cols.transpose(0, 2, 1)
    adjoint = adjoint_cols.transpose(0, 2, 1)
    output = (query.astype(jnp.float32) * conv.astype(jnp.float32)).astype(jnp.bfloat16)
    grad_query = (cotangent.astype(jnp.float32) * conv.astype(jnp.float32)).astype(jnp.bfloat16)
    grad_key = (adjoint.astype(jnp.float32) * value.astype(jnp.float32)).astype(jnp.bfloat16)
    grad_value = (adjoint.astype(jnp.float32) * key_in.astype(jnp.float32)).astype(jnp.bfloat16)
    total_length = query.shape[1] * lax.axis_size("ctx")
    total_batch = seqcount * lax.axis_size("dp")
    scale_factor = 1.0 / math.sqrt(total_batch * total_length * CPG)
    grad_filter = lax.psum_scatter(
        lag_sums * jnp.float32(scale_factor), "dp", scatter_dimension=1, tiled=True
    )
    return (output, grad_query, grad_key, grad_value, grad_filter)


def solution(mesh):
    placed = (
        P("dp", "ctx", None),
        P("dp", "ctx", None),
        P("dp", "ctx", None),
        P("dp", "ctx", None),
        P("ctx", None),
    )
    return jax.shard_map(
        local,
        mesh=mesh,
        in_specs=placed,
        out_specs=(
            P("dp", "ctx", None),
            P("dp", "ctx", None),
            P("dp", "ctx", None),
            P("dp", "ctx", None),
            P("ctx", "dp"),
        ),
        check_vma=False,
    )
```

profile of v0, /device:TPU:0, one launch (start us, length us, event | category | flops | bytes accessed | tf_op | source)
XLA Modules:
  0.0 173.9 jit_solution(15081793441857593579)
XLA Ops:
  7.2 1.1 copy.96
  8.3 1.1 copy.112
  9.5 0.4 copy.151
  9.9 0.5 broadcast.19
  10.4 2.2 %reduce = bf16[1024,128]{1,0:T(8,128)(2,1)S(1)} reduce(bf16[1024,1,128]{2,1,0:T(2,128)(2,1)S(1)} %bitcast.123, bf16[]{:T(256)} %broadcast.19), dimensions={1}, to_apply=%bitcast.114.reduce_sub_computation | reduce | bytes 524290
  12.7 0.8 reshape.86
  13.4 7.3 %all-to-all-start.2 = ((bf16[8,2,8192]{2,1,0:T(2,128)(2,1)}), bf16[8,2,8192]{2,1,0:T(2,128)(2,1)S(1)}, u32[]{:S(2)}, u32[]{:S(2)}) async-start(bf16[8,2,8192]{2,1,0:T(2,128)(2,1)} %reshape.86), calls=%async_computation.2 | async-start | bytes 524288 | tf_op jit(solution)/shard_map/all_to_all | solution.py:114
  20.9 2.0 %copy.144 = bf16[1,4,256,1280]{3,1,2,0:T(4,128)(2,1)S(1)} copy(bf16[1,4,256,1280]{3,2,1,0:T(8,128)(2,1)S(1)} %broadcast_bitcast_fusion) | data formatting | bytes 5242880
  22.9 1.0 slice.53
  23.9 2.5 %reshape.80 = bf16[1309696]{0:T(1024)(128)(2,1)} reshape(bf16[4,327424]{1,0:T(4,128)(2,1)S(1)} %slice.53) | data formatting | bytes 5238784
  26.4 7.6 %reshape.65 = bf16[4,256,1279]{2,1,0:T(8,128)(2,1)S(1)} reshape(bf16[1309696]{0:T(1024)(128)(2,1)} %reshape.80) | data formatting | bytes 5238784 | tf_op jit(solution)/shard_map/reshape | solution.py:38
  34.0 1.6 slice.54
  35.6 2.8 %copy.106 = bf16[4,256,1024]{1,2,0:T(8,128)(2,1)S(1)} copy(bf16[4,256,1024]{2,1,0:T(8,128)(2,1)} %slice.54) | data formatting | bytes 4194304 | tf_op jit(solution)/shard_map/slice | solution.py:38
  38.5 2.4 %copy.107 = bf16[4,256,4,256]{3,1,2,0:T(8,128)(2,1)} copy(bf16[4,256,4,256]{1,3,2,0:T(8,128)(2,1)S(1)} %bitcast.117) | data formatting | bytes 4194304 | tf_op jit(solution)/shard_map/reshape | solution.py:40
  41.9 0.6 copy-done
  42.4 0.8 fusion.10
  43.7 0.6 copy.121
  44.3 2.2 %reduce.1 = bf16[1024,128]{1,0:T(8,128)(2,1)S(1)} reduce(bf16[1024,1,128]{2,1,0:T(2,128)(2,1)S(1)} %bitcast.125, bf16[]{:T(256)} %broadcast.19), dimensions={1}, to_apply=%bitcast.110.reduce_sub_computation | reduce | bytes 524290
  46.5 0.8 reshape.88
  47.3 6.0 %all-to-all-start.3 = ((bf16[8,2,8192]{2,1,0:T(2,128)(2,1)}), bf16[8,2,8192]{2,1,0:T(2,128)(2,1)S(1)}, u32[]{:S(2)}, u32[]{:S(2)}) async-start(bf16[8,2,8192]{2,1,0:T(2,128)(2,1)} %reshape.88), calls=%async_computation.3 | async-start | bytes 524288 | tf_op jit(solution)/shard_map/all_to_all | solution.py:119
  53.7 8.1 %all-to-all-done.3 = bf16[8,2,8192]{2,1,0:T(2,128)(2,1)S(1)} async-done(((bf16[8,2,8192]{2,1,0:T(2,128)(2,1)}), bf16[8,2,8192]{2,1,0:T(2,128)(2,1)S(1)}, u32[]{:S(2)}, u32[]{:S(2)}) %all-to-all-start.3) | async-done | bytes 262176 | tf_op jit(solution)/shard_map/all_to_all | solution.py:119
  62.4 0.8 fusion.24
  63.6 2.2 %reduce.2 = bf16[1024,128]{1,0:T(8,128)(2,1)S(1)} reduce(bf16[1024,1,128]{2,1,0:T(2,128)(2,1)S(1)} %bitcast.126, bf16[]{:T(256)} %broadcast.19), dimensions={1}, to_apply=%bitcast.115.reduce_sub_computation | reduce | bytes 524290
  65.8 0.8 reshape.82
  66.6 4.1 %all-to-all-start = ((bf16[8,2,8192]{2,1,0:T(2,128)(2,1)}), bf16[8,2,8192]{2,1,0:T(2,128)(2,1)}, u32[]{:S(2)}, u32[]{:S(2)}) async-start(bf16[8,2,8192]{2,1,0:T(2,128)(2,1)} %reshape.82), calls=%async_computation | async-start | bytes 524288 | tf_op jit(solution)/shard_map/all_to_all | solution.py:110
  70.7 1.3 rev.7
  72.0 6.9 %all-to-all-done = bf16[8,2,8192]{2,1,0:T(2,128)(2,1)} async-done(((bf16[8,2,8192]{2,1,0:T(2,128)(2,1)}), bf16[8,2,8192]{2,1,0:T(2,128)(2,1)}, u32[]{:S(2)}, u32[]{:S(2)}) %all-to-all-start) | async-done | bytes 262176 | tf_op jit(solution)/shard_map/all_to_all | solution.py:110
  78.9 1.2 reshape.83
  80.5 0.9 stack_reshape_reshape_transpose_reshape.7
  81.3 1.0 copy.103
  82.5 0.5 fusion.13
  84.2 2.2 %reduce.3 = bf16[1024,128]{1,0:T(8,128)(2,1)S(1)} reduce(bf16[1024,1,128]{2,1,0:T(2,128)(2,1)S(1)} %bitcast.124, bf16[]{:T(256)} %broadcast.19), dimensions={1}, to_apply=%bitcast.106.reduce_sub_computation | reduce | bytes 524290
  86.4 0.8 reshape.84
  87.2 3.4 %all-to-all-start.1 = ((bf16[8,2,8192]{2,1,0:T(2,128)(2,1)}), bf16[8,2,8192]{2,1,0:T(2,128)(2,1)S(1)}, u32[]{:S(2)}, u32[]{:S(2)}) async-start(bf16[8,2,8192]{2,1,0:T(2,128)(2,1)} %reshape.84), calls=%async_computation.1 | async-start | bytes 524288 | tf_op jit(solution)/shard_map/all_to_all | solution.py:113
  90.7 2.7 %convolution_bitcast_fusion = f32[4,4,256,256]{2,3,1,0:T(8,128)} fusion(bf16[4,32,4,256,1]{3,2,1,0,4:T(4,128)(2,1)S(1)} %bitcast.131, bf16[4,32,4,1,256]{4,1,3,2,0:T(8,128)(2,1)S(1)} %copy-done.13, bf16[4,32,4,1,256]{4,1,3,2,0:T(8,128)(2,1)S(1)} %copy-done.11, bf16[4,32,4,1,256]{4,1,3,2,0:T(8,128)(2,1)S(1)} %copy-done.9, ...), kind=kOutput, calls=%fused_computation | convolution fusion | flops 270008320 | bytes 5505024 | tf_op jit(solution)/shard_map/gria,gridb->gdab/dot_general | solution.py:86
  93.4 5.3 %copy.143 = f32[4,4,256,256]{3,2,1,0:T(8,128)} copy(f32[4,4,256,256]{2,3,1,0:T(8,128)} %convolution_bitcast_fusion) | data formatting | bytes 8388608
  98.7 6.6 %concatenate.22.clone = f32[4,4,256,512]{3,2,1,0:T(8,128)} pad(f32[4,4,256,256]{3,2,1,0:T(8,128)} %copy.143, f32[]{:T(128)} %constant.4.clone.1), padding=0_0x0_0x0_0x0_256 | pad | bytes 12582916 | tf_op jit(solution)/shard_map/concatenate | solution.py:89
  105.3 9.7 %reshape.67 = f32[4,4,131072]{2,1,0:T(4,128)} reshape(f32[4,4,256,512]{3,2,1,0:T(8,128)} %concatenate.22.clone) | data formatting | bytes 16777216 | tf_op jit(solution)/shard_map/reshape | solution.py:90
  115.0 7.1 %slice.55 = f32[4,4,130816]{2,1,0:T(4,128)} slice(f32[4,4,131072]{2,1,0:T(4,128)} %reshape.67), slice={[0:4], [0:4], [0:130816]} | slice | bytes 16744448 | tf_op jit(solution)/shard_map/slice | solution.py:90
  122.1 11.8 %reshape.68 = f32[4,4,256,511]{3,2,1,0:T(8,128)} reshape(f32[4,4,130816]{2,1,0:T(4,128)} %slice.55) | data formatting | bytes 16744448 | tf_op jit(solution)/shard_map/reshape | solution.py:93
  133.9 4.5 %reduce_sum.9 = f32[4,4,511]{2,1,0:T(4,128)S(1)} reduce(f32[4,4,256,511]{3,2,1,0:T(8,128)} %reshape.68, f32[]{:T(128)} %constant.4.clone.1), dimensions={2}, to_apply=%region_0.0 | reduce | flops 2084880 | bytes 8404932 | tf_op jit(solution)/shard_map/reduce_sum | solution.py:93
  138.8 1.0 copy.140
  139.9 0.9 copy.130
  140.8 0.8 copy.129
  141.6 21.4 %reduce-scatter.4.cloned.1.call-done = f32[256,4]{1,0:T(8,128)} async-done(((f32[1024,4]{1,0:T(8,128)}), f32[256,4]{1,0:T(8,128)}) %reduce-scatter.4.cloned.1.call-update) | async-done | bytes 4112
  163.1 1.6 copy.139
  165.3 0.9 copy.128
  166.2 0.8 copy.127
  (71 shorter events, 5.6 us)
Async XLA Ops:
  7.2 13.5 %copy-start.14 = (bf16[4,1024]{1,0:T(4,128)(2,1)S(1)}, bf16[4,1024]{1,0:T(4,128)(2,1)}, u32[]{:S(2)}) copy-start(bf16[4,1024]{1,0:T(4,128)(2,1)} %param.9) | copy-start | bytes 24580
  13.4 27.4 %all-to-all-start.2 = ((bf16[8,2,8192]{2,1,0:T(2,128)(2,1)}), bf16[8,2,8192]{2,1,0:T(2,128)(2,1)S(1)}, u32[]{:S(2)}, u32[]{:S(2)}) async-start(bf16[8,2,8192]{2,1,0:T(2,128)(2,1)} %reshape.86), calls=%async_computation.2 | async-start | bytes 524288 | tf_op jit(solution)/shard_map/all_to_all | solution.py:114
  40.8 1.6 copy-start
  43.3 10.0 %copy-start.3 = (bf16[1,128,1024]{2,1,0:T(8,128)(2,1)S(1)}, bf16[1,128,1024]{2,1,0:T(8,128)(2,1)}, u32[]{:S(2)}) copy-start(bf16[1,128,1024]{2,1,0:T(8,128)(2,1)} %param.6) | copy-start | bytes 786436
  43.3 10.2 %copy-start.4 = (bf16[1,128,1024]{2,1,0:T(8,128)(2,1)S(1)}, bf16[1,128,1024]{2,1,0:T(8,128)(2,1)}, u32[]{:S(2)}) copy-start(bf16[1,128,1024]{2,1,0:T(8,128)(2,1)} %param.7) | copy-start | bytes 786436
  47.3 14.5 %all-to-all-start.3 = ((bf16[8,2,8192]{2,1,0:T(2,128)(2,1)}), bf16[8,2,8192]{2,1,0:T(2,128)(2,1)S(1)}, u32[]{:S(2)}, u32[]{:S(2)}) async-start(bf16[8,2,8192]{2,1,0:T(2,128)(2,1)} %reshape.88), calls=%async_computation.3 | async-start | bytes 524288 | tf_op jit(solution)/shard_map/all_to_all | solution.py:119
  66.6 12.3 %all-to-all-start = ((bf16[8,2,8192]{2,1,0:T(2,128)(2,1)}), bf16[8,2,8192]{2,1,0:T(2,128)(2,1)}, u32[]{:S(2)}, u32[]{:S(2)}) async-start(bf16[8,2,8192]{2,1,0:T(2,128)(2,1)} %reshape.82), calls=%async_computation | async-start | bytes 524288 | tf_op jit(solution)/shard_map/all_to_all | solution.py:110
  72.0 10.5 %copy-start.1 = (bf16[4,256,4,256]{3,1,2,0:T(8,128)(2,1)S(1)}, bf16[4,256,4,256]{3,1,2,0:T(8,128)(2,1)}, u32[]{:S(2)}) copy-start(bf16[4,256,4,256]{3,1,2,0:T(8,128)(2,1)} %copy.107) | copy-start | bytes 6291460
  82.3 0.7 copy-start.6
  82.5 0.7 copy-start.8
  82.5 0.8 copy-start.10
  82.5 0.9 copy-start.12
  83.3 7.3 %copy-start.5 = (bf16[4,32,4,256]{3,2,1,0:T(4,128)(2,1)S(1)}, bf16[4,32,4,256]{3,2,1,0:T(4,128)(2,1)}, u32[]{:S(2)}) copy-start(bf16[4,32,4,256]{3,2,1,0:T(4,128)(2,1)} %rev.7) | copy-start | bytes 786436
  83.6 7.1 %copy-start.7 = (bf16[4,32,4,1,256]{4,1,3,2,0:T(8,128)(2,1)S(1)}, bf16[4,32,4,1,256]{4,1,3,2,0:T(8,128)(2,1)}, u32[]{:S(2)}) copy-start(bf16[4,32,4,1,256]{4,1,3,2,0:T(8,128)(2,1)} %copy-done.6) | copy-start | bytes 786436
  83.6 7.1 %copy-start.9 = (bf16[4,32,4,1,256]{4,1,3,2,0:T(8,128)(2,1)S(1)}, bf16[4,32,4,1,256]{4,1,3,2,0:T(8,128)(2,1)}, u32[]{:S(2)}) copy-start(bf16[4,32,4,1,256]{4,1,3,2,0:T(8,128)(2,1)} %copy-done.8) | copy-start | bytes 786436
  83.6 7.1 %copy-start.11 = (bf16[4,32,4,1,256]{4,1,3,2,0:T(8,128)(2,1)S(1)}, bf16[4,32,4,1,256]{4,1,3,2,0:T(8,128)(2,1)}, u32[]{:S(2)}) copy-start(bf16[4,32,4,1,256]{4,1,3,2,0:T(8,128)(2,1)} %copy-done.10) | copy-start | bytes 786436
  83.6 7.1 %copy-start.13 = (bf16[4,32,4,1,256]{4,1,3,2,0:T(8,128)(2,1)S(1)}, bf16[4,32,4,1,256]{4,1,3,2,0:T(8,128)(2,1)}, u32[]{:S(2)}) copy-start(bf16[4,32,4,1,256]{4,1,3,2,0:T(8,128)(2,1)} %copy-done.12) | copy-start | bytes 786436
  87.2 77.5 %all-to-all-start.1 = ((bf16[8,2,8192]{2,1,0:T(2,128)(2,1)}), bf16[8,2,8192]{2,1,0:T(2,128)(2,1)S(1)}, u32[]{:S(2)}, u32[]{:S(2)}) async-start(bf16[8,2,8192]{2,1,0:T(2,128)(2,1)} %reshape.84), calls=%async_computation.1 | async-start | bytes 524288 | tf_op jit(solution)/shard_map/all_to_all | solution.py:113
  90.6 72.5 %reduce-scatter.4.cloned.1.call-start = ((), (), s32[]{:S(2)}) async-start(), calls=%async_computation.5 | async-start | bytes 655360
  133.9 6.1 %copy-start.2 = (bf16[1,128,1024]{1,2,0:T(8,128)(2,1)S(1)}, bf16[1,128,1024]{1,2,0:T(8,128)(2,1)}, u32[]{:S(2)}) copy-start(bf16[1,128,1024]{1,2,0:T(8,128)(2,1)} %get-tuple-element.20) | copy-start | bytes 786436
Sparse Core Ops, SparseCore 0:
  140.0 22.9 reduce-scatter.3
where the time goes:
time: 175 us; the launch traced here: 174 us
  local copies, waits for them, and re-layouts  83.5 us (48%)
  waiting for transfers between devices  36.5 us (21%)
  starting transfers between devices  20.8 us (12%)
  between operations  14.6 us (8%)
  other arithmetic  14.5 us (8%)
  matrix products  4.05 us (2%)
    unnamed x55, local copies, waits for them, and re-layouts  25.1 us
    unnamed x2, waiting for transfers between devices  21.4 us
    reshape x1, local copies, waits for them, and re-layouts, filter_lags(): padded.reshape(groups, nblocks, blocksize, 2 * blocksize - 1).sum(axis=2)  11.8 us
    reshape x1, local copies, waits for them, and re-layouts, filter_lags(): padded.reshape(groups, nblocks, 2 * blocksize * blocksize)  9.69 us
    unnamed x4, other arithmetic  8.84 us
    all_to_all x1, waiting for transfers between devices, local(): lax.all_to_all(adjoint_own, 'ctx', split_axis=2, concat_axis=1, tiled=True)  8.14 us
    reshape x1, local copies, waits for them, and re-layouts, band_blocks(): shifted = tiled.reshape(groups, blocksize, width - 1)[:, :, :length]  7.6 us
    all_to_all x1, starting transfers between devices, local(): lax.all_to_all(gradin_cols, 'ctx', split_axis=1, concat_axis=2, tiled=True)  7.25 us
  transfers between devices with their start and end apart: 5, of which 3 were waited for; matrix products, arithmetic and copies ran while one was open for 43% of the time, Pallas kernels for 0%

commit v1 on v0

v1 whole, which is shorter than its diff:
```python
import functools
import math

import jax
import jax.numpy as jnp
from jax import lax
from jax.experimental import pallas as pl
from jax.experimental.pallas import tpu as pltpu
from jax.sharding import PartitionSpec as P

CPG = 32
MESH = pl.DeviceIdType.MESH
F32 = jnp.float32
BF16 = jnp.bfloat16


def dot(a, b, contract=((1,), (0,))):
    return lax.dot_general(a, b, (contract, ((), ())), preferred_element_type=F32)


def kernel(
    n, ndp, scale,
    q_ref, k_ref, v_ref, ct_ref, f_ref,
    conv_ref, adj_ref, gf_ref,
    send, recv, strips, masked, retc, reta, backc, backa, lhs, rhs, lags, gsend, grecv,
    send_sem, recv_sem, csend_sem, crecv_sem, asend_sem, arecv_sem, gsend_sem, grecv_sem,
):
    me = lax.axis_index("ctx")
    row = lax.axis_index("dp")
    piece, channels = q_ref.shape
    width = channels // n
    groups, length = f_ref.shape
    part = length // ndp

    barrier = pltpu.get_barrier_semaphore()
    for step in range(1, n):
        pl.semaphore_signal(
            barrier, inc=1, device_id={"ctx": lax.rem(me + step, n)}, device_id_type=MESH
        )
    for step in range(1, ndp):
        pl.semaphore_signal(
            barrier, inc=1, device_id={"dp": lax.rem(row + step, ndp)}, device_id_type=MESH
        )

    at_row = lax.broadcasted_iota(jnp.int32, (piece, piece), 0)
    at_col = lax.broadcasted_iota(jnp.int32, (piece, piece), 1)
    flip = jnp.where(at_row + at_col == piece - 1, 1.0, 0.0).astype(BF16)

    mixed = (k_ref[...].astype(F32) * v_ref[...].astype(F32)).astype(BF16)
    turned = dot(flip, mixed).astype(BF16)
    gradin = (ct_ref[...].astype(F32) * q_ref[...].astype(F32)).astype(BF16)
    for owner in range(n):
        span = slice(owner * width, (owner + 1) * width)
        send[owner, :, :width] = turned[:, span]
        send[owner, :, width:] = gradin[:, span]
    pl.semaphore_wait(barrier, n - 1 + ndp - 1)

    def outward(step):
        owner = lax.rem(me + step, n)
        return pltpu.make_async_remote_copy(
            src_ref=send.at[owner], dst_ref=recv.at[me],
            send_sem=send_sem.at[owner], recv_sem=recv_sem.at[me],
            device_id={"ctx": owner}, device_id_type=MESH,
        )

    def inward(source):
        return pltpu.make_async_remote_copy(
            src_ref=send.at[source], dst_ref=recv.at[source],
            send_sem=send_sem.at[source], recv_sem=recv_sem.at[source],
            device_id={"ctx": source}, device_id_type=MESH,
        )

    for step in range(1, n):
        outward(step).start()
    recv[me] = send[me]

    filters = f_ref[...].astype(F32)
    padded = jnp.concatenate([filters, jnp.zeros((groups, piece), F32)], axis=1)
    for g in range(groups):
        spread = jnp.broadcast_to(padded[g : g + 1], (piece, length + piece))
        strip = pltpu.roll(spread, 0, 1, stride=1, stride_axis=0).astype(BF16)
        strips[g, :piece] = strip[:, :length]
        strips[g, piece:, :piece] = jnp.zeros((piece, piece), BF16)
        strips[g, piece:, piece:] = strip[:, : length - piece]

    channel = lax.broadcasted_iota(jnp.int32, (1, width), 1) // CPG
    picks = [jnp.where(channel == g, 1.0, 0.0).astype(BF16) for g in range(groups)]

    for step in range(1, n):
        inward(lax.rem(me + step, n)).wait_recv()

    for block in range(n):
        rows = slice(block * piece, (block + 1) * piece)
        signal = recv[n - 1 - block, :, :width]
        grads = recv[block, :, width:]
        for g in range(groups):
            masked[g, rows, :width] = signal * picks[g]
            masked[g, rows, width:] = grads * picks[g]

    def give(block, values, staged, landed, out_sem, in_sem):
        def copy():
            return pltpu.make_async_remote_copy(
                src_ref=staged.at[block], dst_ref=landed.at[me],
                send_sem=out_sem.at[block], recv_sem=in_sem.at[me],
                device_id={"ctx": jnp.int32(block)}, device_id_type=MESH,
            )

        @pl.when(me == block)
        def _():
            landed[me] = values

        @pl.when(me != block)
        def _():
            staged[block] = values
            copy().start()

    for pair in range(n // 2):
        first = 2 * pair * piece
        total = dot(strips[0, :, : length - first], masked[0, first:, :])
        for g in range(1, groups):
            total += dot(strips[g, :, : length - first], masked[g, first:, :])
        total = total.astype(BF16)
        for half in range(2):
            rows = slice(half * piece, (half + 1) * piece)
            block = 2 * pair + half
            give(n - 1 - block, total[rows, :width], retc, backc, csend_sem, crecv_sem)
            give(block, total[rows, width:], reta, backa, asend_sem, arecv_sem)

    for block in range(n):
        span = slice(block * width, (block + 1) * width)
        for g in range(groups):
            lhs[g * piece : (g + 1) * piece, span] = recv[block, :, :width] * picks[g]
        rhs[:piece, span] = recv[block, :, width:]
        if block + 1 < n:
            rhs[piece:, span] = recv[block + 1, :, width:]
        else:
            rhs[piece:, span] = jnp.zeros((piece, width), BF16)
    lags[:, length:] = jnp.zeros((groups * piece, piece), F32)
    for pair in range(n // 2):
        first = 2 * pair * piece
        depth = (n - 2 * pair) * width
        lags[:, first : first + 2 * piece] = dot(
            lhs[:, :depth], rhs[:, 2 * pair * width :], ((1,), (1,))
        )
    for g in range(groups):
        skewed = pltpu.roll(lags[g * piece : (g + 1) * piece, :], 1, 1, stride=1, stride_axis=0)
        sums = jnp.sum(skewed, axis=0, keepdims=True)[:, piece:] * F32(scale)
        for to in range(ndp):
            gsend[to, g : g + 1, :] = sums[:, to * part : (to + 1) * part]

    def terms(to, at):
        return pltpu.make_async_remote_copy(
            src_ref=gsend.at[to], dst_ref=grecv.at[at],
            send_sem=gsend_sem.at[to], recv_sem=grecv_sem.at[at],
            device_id={"dp": to}, device_id_type=MESH,
        )

    for step in range(1, ndp):
        terms(lax.rem(row + step, ndp), row).start()
    grecv[row] = gsend[row]

    for owner in range(n):
        span = slice(owner * width, (owner + 1) * width)

        @pl.when(me != owner)
        def _():
            pltpu.make_async_remote_copy(
                src_ref=retc.at[owner], dst_ref=backc.at[owner],
                send_sem=csend_sem.at[owner], recv_sem=crecv_sem.at[owner],
                device_id={"ctx": jnp.int32(owner)}, device_id_type=MESH,
            ).wait()
            pltpu.make_async_remote_copy(
                src_ref=reta.at[owner], dst_ref=backa.at[owner],
                send_sem=asend_sem.at[owner], recv_sem=arecv_sem.at[owner],
                device_id={"ctx": jnp.int32(owner)}, device_id_type=MESH,
            ).wait()

        conv_ref[:, span] = dot(flip, backc[owner]).astype(BF16)
        adj_ref[:, span] = backa[owner]

    for step in range(1, ndp):
        other = lax.rem(row + step, ndp)
        terms(other, other).wait()
    gathered = grecv[0]
    for at in range(1, ndp):
        gathered += grecv[at]
    gf_ref[...] = gathered

    for step in range(1, n):
        outward(step).wait_send()


def solution(mesh):
    n, ndp = mesh.shape["ctx"], mesh.shape["dp"]

    def local(query, key_in, value, cotangent, filters):
        count, piece, channels = query.shape
        groups, length = filters.shape
        width = channels // n
        part = length // ndp
        scale = 1.0 / math.sqrt(count * ndp * length * CPG)
        q, k, v, ct = (x.reshape(piece, channels) for x in (query, key_in, value, cotangent))
        vmem = pl.BlockSpec(memory_space=pltpu.VMEM)
        dma = pltpu.SemaphoreType.DMA
        conv, adjoint, grad_filter = pl.pallas_call(
            functools.partial(kernel, n, ndp, scale),
            out_shape=(
                jax.ShapeDtypeStruct((piece, channels), BF16),
                jax.ShapeDtypeStruct((piece, channels), BF16),
                jax.ShapeDtypeStruct((groups, part), F32),
            ),
            in_specs=[vmem] * 5,
            out_specs=(vmem, vmem, vmem),
            scratch_shapes=[
                pltpu.VMEM((n, piece, 2 * width), BF16),
                pltpu.VMEM((n, piece, 2 * width), BF16),
                pltpu.VMEM((groups, 2 * piece, length), BF16),
                pltpu.VMEM((groups, length, 2 * width), BF16),
                pltpu.VMEM((n, piece, width), BF16),
                pltpu.VMEM((n, piece, width), BF16),
                pltpu.VMEM((n, piece, width), BF16),
                pltpu.VMEM((n, piece, width), BF16),
                pltpu.VMEM((groups * piece, n * width), BF16),
                pltpu.VMEM((2 * piece, n * width), BF16),
                pltpu.VMEM((groups * piece, length + piece), F32),
                pltpu.VMEM((ndp, groups, part), F32),
                pltpu.VMEM((ndp, groups, part), F32),
                dma((n,)), dma((n,)), dma((n,)), dma((n,)), dma((n,)), dma((n,)),
                dma((ndp,)), dma((ndp,)),
            ],
            compiler_params=pltpu.CompilerParams(
                collective_id=0, has_side_effects=True, vmem_limit_bytes=40 * 1024 * 1024
            ),
            cost_estimate=pl.CostEstimate(
                flops=3 * channels * length * length // n,
                bytes_accessed=12 * piece * channels,
                transcendentals=0,
            ),
        )(q, k, v, ct, filters)
        conv = conv.reshape(query.shape).astype(F32)
        adjoint = adjoint.reshape(query.shape).astype(F32)
        output = (query.astype(F32) * conv).astype(BF16)
        grad_query = (cotangent.astype(F32) * conv).astype(BF16)
        grad_key = (adjoint * value.astype(F32)).astype(BF16)
        grad_value = (adjoint * key_in.astype(F32)).astype(BF16)
        return output, grad_query, grad_key, grad_value, grad_filter

    signal = P("dp", "ctx", None)
    return jax.shard_map(
        local,
        mesh=mesh,
        in_specs=(signal, signal, signal, signal, P("ctx", None)),
        out_specs=(signal, signal, signal, signal, P("ctx", "dp")),
        check_vma=False,
    )
```

time: 175 us -> 41.3 us (0.24)
  local copies, waits for them, and re-layouts: 83.5 us -> 5.08 us
  waiting for transfers between devices: 36.5 us -> 0 us
  Pallas kernels: 0 us -> 34.1 us
  starting transfers between devices: 20.8 us -> 0 us
  between operations: 14.6 us -> 0.65 us
  other arithmetic: 14.5 us -> 1.22 us
  matrix products: 4.05 us -> 0 us
    pallas_call x0 -> x1, Pallas kernels: none -> 34.1 us  [local(): pl.pallas_call(functools.partial(kernel, n, ndp, scale), out_shape=(jax.S...]
    reshape x4 -> x0, local copies, waits for them, and re-layouts: 31.4 us -> none  [the longest x1 11.8 us: filter_lags(): padded.reshape(groups, nblocks, blocksize, 2 * blocksize - 1).sum(axis=2)]
    unnamed x2 -> x0, waiting for transfers between devices: 21.4 us -> none
    all_to_all x4 -> x0, starting transfers between devices: 20.7 us -> none  [the longest x1 7.25 us: local(): lax.all_to_all(gradin_cols, 'ctx', split_axis=1, concat_axis=2, tiled=True)]
    unnamed x55 -> x11, local copies, waits for them, and re-layouts: 25.1 us -> 5.08 us
    all_to_all x4 -> x0, waiting for transfers between devices: 15.1 us -> none  [the longest x1 8.14 us: local(): lax.all_to_all(adjoint_own, 'ctx', split_axis=2, concat_axis=1, tiled=True)]
    slice x7 -> x0, local copies, waits for them, and re-layouts: 12.8 us -> none  [the longest x1 7.13 us: filter_lags(): padded.reshape(groups, nblocks, 2 * blocksize * blocksize)]
    unnamed x4 -> x0, other arithmetic: 8.84 us -> none
  transfers between devices with their start and end apart: 5 -> 0, of which waited for: 3 -> 0; matrix products, arithmetic and copies ran while one was open for 43% -> 0% of each run, Pallas kernels for 0% -> 0%
where the time goes in v1:
time: 41.3 us; the launch traced here: 41.1 us
  Pallas kernels  34.1 us (83%)
  local copies, waits for them, and re-layouts  5.08 us (12%)
  other arithmetic  1.22 us (3%)
  between operations  0.65 us (2%)
    pallas_call x1, Pallas kernels, local(): pl.pallas_call(functools.partial(kernel, n, ndp, scale), out_shape=(jax.S...  34.1 us
    unnamed x11, local copies, waits for them, and re-layouts  5.08 us
    convert_element_type x1, other arithmetic, local(): grad_query = (cotangent.astype(F32) * conv).astype(BF16)  1.22 us

profile of v1, /device:TPU:0, one launch (start us, length us, event | category | flops | bytes accessed | tf_op | source)
XLA Modules:
  0.0 41.1 jit_solution(13606638149040427277)
XLA Ops:
  0.6 0.0 copy-start
  0.6 0.9 %copy-done = bf16[1,128,1024]{2,1,0:T(8,128)(2,1)S(1)} copy-done((bf16[1,128,1024]{2,1,0:T(8,128)(2,1)S(1)}, bf16[1,128,1024]{2,1,0:T(8,128)(2,1)}, u32[]{:S(2)}) %copy-start) | copy-done | bytes 262168
  1.6 0.0 copy-start.1
  1.6 0.9 %copy-done.1 = bf16[1,128,1024]{2,1,0:T(8,128)(2,1)S(1)} copy-done((bf16[1,128,1024]{2,1,0:T(8,128)(2,1)S(1)}, bf16[1,128,1024]{2,1,0:T(8,128)(2,1)}, u32[]{:S(2)}) %copy-start.1) | copy-done | bytes 262168
  2.5 0.0 copy-start.2
  2.5 0.9 %copy-done.2 = bf16[1,128,1024]{2,1,0:T(8,128)(2,1)S(1)} copy-done((bf16[1,128,1024]{2,1,0:T(8,128)(2,1)S(1)}, bf16[1,128,1024]{2,1,0:T(8,128)(2,1)}, u32[]{:S(2)}) %copy-start.2) | copy-done | bytes 262168
  3.5 0.0 copy-start.3
  3.5 0.9 %copy-done.3 = bf16[1,128,1024]{2,1,0:T(8,128)(2,1)S(1)} copy-done((bf16[1,128,1024]{2,1,0:T(8,128)(2,1)S(1)}, bf16[1,128,1024]{2,1,0:T(8,128)(2,1)}, u32[]{:S(2)}) %copy-start.3) | copy-done | bytes 262168
  4.4 0.0 copy-start.4
  4.4 0.7 %copy-done.4 = bf16[4,1024]{1,0:T(4,128)(2,1)S(1)} copy-done((bf16[4,1024]{1,0:T(4,128)(2,1)S(1)}, bf16[4,1024]{1,0:T(4,128)(2,1)}, u32[]{:S(2)}) %copy-start.4) | copy-done | bytes 8216
  5.1 34.1 %shard_map.92 = (bf16[128,1024]{1,0:T(8,128)(2,1)S(1)}, bf16[128,1024]{1,0:T(8,128)(2,1)S(1)}, f32[4,256]{1,0:T(4,128)S(1)}) custom-call(bf16[128,1024]{1,0:T(8,128)(2,1)S(1)} %bitcast.13, bf16[128,1024]{1,0:T(8,128)(2,1)S(1)} %bitcast.14, bf16[128,1024]{1,0:T(8,128)(2,1)S(1)} %bitcast.15, bf16[128,1024]{1,0:T(8,128)(2,1)S(1)} %bitcast.12, ...), custom_call_target="tpu_custom_call" | custom-call | flops 402653184 | bytes 1572864 | tf_op jit(solution)/shard_map/pallas_call | solution.py:205
  39.2 1.2 %fusion.1 = (bf16[1,128,1024]{2,1,0:T(8,128)(2,1)}, bf16[1,128,1024]{2,1,0:T(8,128)(2,1)}, bf16[1,128,1024]{2,1,0:T(8,128)(2,1)}, bf16[1,128,1024]{2,1,0:T(8,128)(2,1)}) fusion(bf16[1,128,1024]{2,1,0:T(8,128)(2,1)S(1)} %copy-done, bf16[128,1024]{1,0:T(8,128)(2,1)S(1)} %get-tuple-element.8, bf16[1,128,1024]{2,1,0:T(8,128)(2,1)S(1)} %copy-done.1, ...), kind=kLoop, calls=%fused_computation.5 | loop fusion | flops 1835008 | bytes 2621440 | tf_op jit(solution)/shard_map/convert_element_type | solution.py:243
  40.5 0.6 %copy.11 = f32[4,256]{1,0:T(4,128)} copy(f32[4,256]{1,0:T(4,128)S(1)} %get-tuple-element.26) | data formatting | bytes 8192
Async XLA Ops:
  0.6 1.0 %copy-start = (bf16[1,128,1024]{2,1,0:T(8,128)(2,1)S(1)}, bf16[1,128,1024]{2,1,0:T(8,128)(2,1)}, u32[]{:S(2)}) copy-start(bf16[1,128,1024]{2,1,0:T(8,128)(2,1)} %param.8) | copy-start | bytes 786436
  1.6 0.9 %copy-start.1 = (bf16[1,128,1024]{2,1,0:T(8,128)(2,1)S(1)}, bf16[1,128,1024]{2,1,0:T(8,128)(2,1)}, u32[]{:S(2)}) copy-start(bf16[1,128,1024]{2,1,0:T(8,128)(2,1)} %param.5) | copy-start | bytes 786436
  2.5 0.9 %copy-start.2 = (bf16[1,128,1024]{2,1,0:T(8,128)(2,1)S(1)}, bf16[1,128,1024]{2,1,0:T(8,128)(2,1)}, u32[]{:S(2)}) copy-start(bf16[1,128,1024]{2,1,0:T(8,128)(2,1)} %param.6) | copy-start | bytes 786436
  3.5 0.9 %copy-start.3 = (bf16[1,128,1024]{2,1,0:T(8,128)(2,1)S(1)}, bf16[1,128,1024]{2,1,0:T(8,128)(2,1)}, u32[]{:S(2)}) copy-start(bf16[1,128,1024]{2,1,0:T(8,128)(2,1)} %param.7) | copy-start | bytes 786436
  4.4 0.7 %copy-start.4 = (bf16[4,1024]{1,0:T(4,128)(2,1)S(1)}, bf16[4,1024]{1,0:T(4,128)(2,1)}, u32[]{:S(2)}) copy-start(bf16[4,1024]{1,0:T(4,128)(2,1)} %f_ref.1) | copy-start | bytes 24580

commit v2 on v1

v2 whole, which is shorter than its diff:
```python
import functools
import math

import jax
import jax.numpy as jnp
from jax import lax
from jax.experimental import pallas as pl
from jax.experimental.pallas import tpu as pltpu
from jax.sharding import PartitionSpec as P

CPG = 32
MESH = pl.DeviceIdType.MESH
F32 = jnp.float32
BF16 = jnp.bfloat16


def dot(a, b, contract=((1,), (0,))):
    return lax.dot_general(a, b, (contract, ((), ())), preferred_element_type=F32)


def kernel(
    n, ndp, scale,
    q_hbm, k_hbm, v_hbm, ct_hbm, f_hbm,
    conv_ref, adj_ref, gf_ref,
    q_ref, k_ref, v_ref, ct_ref, f_ref, load_sem,
    slong, sshort, rlong, rshort, rcross, fpair, strips, mlong, mshort,
    tlong, tshort, backl, backs, lhs, rhs, lags, gsend, grecv,
    slong_sem, sshort_sem, scross_sem, rlong_sem, rshort_sem, rcross_sem, f_sem,
    tlong_sem, tshort_sem, backl_sem, backs_sem, gsend_sem, grecv_sem,
):
    me = lax.axis_index("ctx")
    row = lax.axis_index("dp")
    hn = n // 2
    half = me // hn
    rank = me - half * hn
    partner = (1 - half) * hn + rank
    low = half == 0
    piece, channels = q_ref.shape
    width = channels // n
    groups, length = f_ref.shape
    part = length // ndp
    reach = hn * piece
    long_slot = (1 - half) * rank + half * (hn - 1 - rank)
    short_slot = hn - 1 - long_slot

    def choose(a, b):
        return jnp.where(low, a.astype(F32), b.astype(F32)).astype(BF16)

    loads = [
        pltpu.make_async_copy(hbm, ref, load_sem.at[at])
        for at, (hbm, ref) in enumerate(
            [(k_hbm, k_ref), (v_hbm, v_ref), (ct_hbm, ct_ref), (q_hbm, q_ref), (f_hbm, f_ref)]
        )
    ]
    for load in loads:
        load.start()
    barrier = pltpu.get_barrier_semaphore()
    for step in range(1, n):
        pl.semaphore_signal(
            barrier, inc=1, device_id={"ctx": lax.rem(me + step, n)}, device_id_type=MESH
        )
    for step in range(1, ndp):
        to = lax.rem(row + step, ndp)
        pl.semaphore_signal(barrier, inc=1, device_id={"dp": to}, device_id_type=MESH)
        pl.semaphore_signal(
            barrier, inc=1, device_id={"ctx": partner, "dp": to}, device_id_type=MESH
        )

    at_row = lax.broadcasted_iota(jnp.int32, (piece, piece), 0)
    at_col = lax.broadcasted_iota(jnp.int32, (piece, piece), 1)
    flip = jnp.where(at_row + at_col == piece - 1, 1.0, 0.0).astype(BF16)

    loads[0].wait()
    loads[1].wait()
    mixed = (k_ref[...].astype(F32) * v_ref[...].astype(F32)).astype(BF16)
    turned = dot(flip, mixed).astype(BF16)
    loads[2].wait()
    loads[3].wait()
    gradin = (ct_ref[...].astype(F32) * q_ref[...].astype(F32)).astype(BF16)
    long = choose(gradin, turned)
    short = choose(turned, gradin)
    for owner in range(hn):
        for block in range(2):
            to = slice(block * width, (block + 1) * width)
            at = (owner + block * hn) * width
            slong[owner, :, to] = long[:, at : at + width]
            sshort[owner, :, to] = short[:, at : at + width]
    loads[4].wait()
    fpair[half] = f_ref[...].astype(F32)
    pl.semaphore_wait(barrier, n - 1 + 2 * (ndp - 1))

    def copy(src, dst, out_sem, in_sem, to):
        return pltpu.make_async_remote_copy(
            src_ref=src, dst_ref=dst, send_sem=out_sem, recv_sem=in_sem,
            device_id={"ctx": to}, device_id_type=MESH,
        )

    filters_copy = copy(fpair.at[half], fpair.at[half], f_sem.at[0], f_sem.at[1], partner)
    filters_copy.start()
    outward = []
    for step in range(1, hn):
        owner = lax.rem(rank + step, hn)
        outward.append(copy(
            sshort.at[owner], rshort.at[short_slot], sshort_sem.at[owner],
            rshort_sem.at[short_slot], half * hn + owner,
        ))
    for step in range(hn):
        owner = lax.rem(rank + step, hn)
        outward.append(copy(
            sshort.at[owner], rcross.at[short_slot], scross_sem.at[owner],
            rcross_sem.at[short_slot], (1 - half) * hn + owner,
        ))
    for step in range(1, hn):
        owner = lax.rem(rank + step, hn)
        outward.append(copy(
            slong.at[owner], rlong.at[long_slot], slong_sem.at[owner],
            rlong_sem.at[long_slot], half * hn + owner,
        ))
    for each in outward:
        each.start()
    rlong[long_slot] = slong[rank]
    rshort[short_slot] = sshort[rank]

    copy(
        fpair.at[1 - half], fpair.at[1 - half], f_sem.at[0], f_sem.at[1], partner
    ).wait_recv()
    for g in range(2 * groups):
        line = fpair[g // groups, g % groups : g % groups + 1, :]
        line = jnp.concatenate([line, jnp.zeros((1, piece), F32)], axis=1)
        spread = jnp.broadcast_to(line, (piece, length + piece))
        strip = pltpu.roll(spread, 0, 1, stride=1, stride_axis=0).astype(BF16)
        strips[g, :piece] = strip[:, :length]
        strips[g, piece:, :piece] = jnp.zeros((piece, piece), BF16)
        strips[g, piece:, piece:] = strip[:, : length - piece]

    channel = lax.broadcasted_iota(jnp.int32, (1, width), 1) // CPG
    picks = [jnp.where(channel == g, 1.0, 0.0).astype(BF16) for g in range(groups)]

    def arrive(landed, sem, slot):
        copy(landed.at[slot], landed.at[slot], slong_sem.at[0], sem.at[slot], partner).wait_recv()

    def spread_out(landed, slot, masked, at):
        for g in range(2 * groups):
            side = (g // groups) * width
            masked[g, at * piece : (at + 1) * piece, :] = (
                landed[slot, :, side : side + width] * picks[g % groups]
            )

    def convolve(masked, depth, staged, landed, out_sem, in_sem, own_slot, mirrored):
        for pair in range(hn // 2):
            first = 2 * pair * piece
            for block in range(2):
                total = None
                for g in range(block * groups, (block + 1) * groups):
                    term = dot(strips[g, :, : depth - first], masked[g, first:, :])
                    total = term if total is None else total + term
                total = total.astype(BF16)
                for at in range(2):
                    staged[2 * pair + at, :, block * width : (block + 1) * width] = total[
                        at * piece : (at + 1) * piece
                    ]
            for at in range(2):
                slot = 2 * pair + at
                source = mirrored * (hn - 1 - slot) + (1 - mirrored) * slot

                @pl.when(own_slot == slot)
                def _():
                    landed[rank] = staged[slot]

                @pl.when(own_slot != slot)
                def _():
                    copy(
                        staged.at[slot], landed.at[rank], out_sem.at[slot], in_sem.at[rank],
                        half * hn + source,
                    ).start()

    for slot in range(hn):
        @pl.when(slot != short_slot)
        def _():
            arrive(rshort, rshort_sem, slot)
        spread_out(rshort, slot, mshort, slot)
    convolve(mshort, reach, tshort, backs, tshort_sem, backs_sem, short_slot, 1 - half)

    for slot in range(hn):
        arrive(rcross, rcross_sem, slot)
        spread_out(rcross, slot, mlong, hn + slot)
    for slot in range(hn):
        @pl.when(slot != long_slot)
        def _():
            arrive(rlong, rlong_sem, slot)
        spread_out(rlong, slot, mlong, slot)
    convolve(mlong, 2 * reach, tlong, backl, tlong_sem, backl_sem, long_slot, half)

    def lanes(values, role):
        left, right = values[:, :width], values[:, width:]
        return choose(left, right) if role == 0 else choose(right, left)

    def fill(at, values):
        rhs[:piece, at * width : (at + 1) * width] = values
        if at > 0:
            rhs[piece:, (at - 1) * width : at * width] = values

    def fill_lhs(at, values):
        for g in range(groups):
            lhs[g * piece : (g + 1) * piece, at * width : (at + 1) * width] = values * picks[g]

    none = jnp.zeros((piece, width), BF16)

    def lag_sums(g, extent):
        rows = slice(g * piece, (g + 1) * piece)
        skewed = pltpu.roll(lags[rows, : extent + piece], 1, 1, stride=1, stride_axis=0)
        return jnp.sum(skewed, axis=0, keepdims=True)[:, piece:] * F32(scale)

    def keep(role, g, sums, extent):
        for to in range(ndp):
            if to * part < extent:
                gsend[role, to, g : g + 1, :] = sums[:, to * part : (to + 1) * part]
            else:
                gsend[role, to, g : g + 1, :] = jnp.zeros((1, part), F32)

    def terms(role, to, at):
        return pltpu.make_async_remote_copy(
            src_ref=gsend.at[role, to], dst_ref=grecv.at[role, at],
            send_sem=gsend_sem.at[role, to], recv_sem=grecv_sem.at[role, at],
            device_id={"ctx": me if role == 0 else partner, "dp": to}, device_id_type=MESH,
        )

    for role in (1, 0):
        for at in range(hn):
            fill_lhs(at, lanes(choose(rshort[hn - 1 - at], rlong[hn - 1 - at]), role))
            fill(at, lanes(choose(rlong[at], rshort[at]), role))
        fill(hn, none)
        for pair in range(hn // 2):
            first = 2 * pair
            lags[:, first * piece : (first + 2) * piece] = dot(
                lhs[:, : (hn - first) * width], rhs[:, first * width : hn * width], ((1,), (1,))
            )
        if role == 1:
            lags[:, reach : reach + piece] = jnp.zeros((groups * piece, piece), F32)
            for g in range(groups):
                keep(1, g, lag_sums(g, reach), reach)
            for step in range(ndp):
                to = lax.rem(row + step, ndp)
                terms(1, to, row).start()
    for at in range(hn):
        fill_lhs(at, lanes(choose(rshort[hn - 1 - at], rcross[hn - 1 - at]), 0))
    for at in range(n + hn):
        if hn <= at < n:
            fill(at, lanes(choose(rcross[at - hn], rshort[at - hn]), 0))
        else:
            fill(at, none)
    fill_last = slice((n + hn - 1) * width, (n + hn) * width)
    rhs[piece:, fill_last] = none
    lags[:, reach:] = jnp.zeros((groups * piece, length - reach + piece), F32)
    for pair in range(hn):
        first = 2 * pair
        lags[:, first * piece : (first + 2) * piece] += dot(
            lhs[...], rhs[:, first * width : (first + hn) * width], ((1,), (1,))
        )
    for g in range(groups):
        keep(0, g, lag_sums(g, length), length)
    for step in range(1, ndp):
        terms(0, lax.rem(row + step, ndp), row).start()
    grecv[0, row] = gsend[0, row]

    for owner in range(hn):
        @pl.when(rank != owner)
        def _():
            arrive(backs, backs_sem, owner)
            arrive(backl, backl_sem, owner)
        conv = dot(flip, choose(backs[owner], backl[owner])).astype(BF16)
        adjoint = choose(backl[owner], backs[owner])
        for block in range(2):
            side = slice(block * width, (block + 1) * width)
            at = (owner + block * hn) * width
            conv_ref[:, at : at + width] = conv[:, side]
            adj_ref[:, at : at + width] = adjoint[:, side]

    for step in range(1, ndp):
        other = lax.rem(row + step, ndp)
        terms(0, other, other).wait()
    for step in range(ndp):
        other = lax.rem(row + step, ndp)
        terms(1, other, other).wait()
    gathered = grecv[0, 0]
    for at in range(1, 2 * ndp):
        gathered += grecv[at // ndp, at % ndp]
    gf_ref[...] = gathered

    filters_copy.wait_send()
    for each in outward:
        each.wait_send()
    for slot in range(hn):
        @pl.when(slot != short_slot)
        def _():
            copy(
                tshort.at[slot], backs.at[rank], tshort_sem.at[slot], backs_sem.at[rank], partner
            ).wait_send()

        @pl.when(slot != long_slot)
        def _():
            copy(
                tlong.at[slot], backl.at[rank], tlong_sem.at[slot], backl_sem.at[rank], partner
            ).wait_send()


def solution(mesh):
    n, ndp = mesh.shape["ctx"], mesh.shape["dp"]

    def local(query, key_in, value, cotangent, filters):
        count, piece, channels = query.shape
        groups, length = filters.shape
        hn, width = n // 2, channels // n
        part = length // ndp
        scale = 1.0 / math.sqrt(count * ndp * length * CPG)
        q, k, v, ct = (x.reshape(piece, channels) for x in (query, key_in, value, cotangent))
        vmem = pl.BlockSpec(memory_space=pltpu.VMEM)
        dma = pltpu.SemaphoreType.DMA
        conv, adjoint, grad_filter = pl.pallas_call(
            functools.partial(kernel, n, ndp, scale),
            out_shape=(
                jax.ShapeDtypeStruct((piece, channels), BF16),
                jax.ShapeDtypeStruct((piece, channels), BF16),
                jax.ShapeDtypeStruct((groups, part), F32),
            ),
            in_specs=[pl.BlockSpec(memory_space=pltpu.HBM)] * 5,
            out_specs=(vmem, vmem, vmem),
            scratch_shapes=[
                pltpu.VMEM((piece, channels), BF16),
                pltpu.VMEM((piece, channels), BF16),
                pltpu.VMEM((piece, channels), BF16),
                pltpu.VMEM((piece, channels), BF16),
                pltpu.VMEM((groups, length), BF16),
                dma((5,)),
                *[pltpu.VMEM((hn, piece, 2 * width), BF16) for _ in range(5)],
                pltpu.VMEM((2, groups, length), F32),
                pltpu.VMEM((2 * groups, 2 * piece, length), BF16),
                pltpu.VMEM((2 * groups, length, width), BF16),
                pltpu.VMEM((2 * groups, length // 2, width), BF16),
                *[pltpu.VMEM((hn, piece, 2 * width), BF16) for _ in range(4)],
                pltpu.VMEM((groups * piece, hn * width), BF16),
                pltpu.VMEM((2 * piece, (n + hn) * width), BF16),
                pltpu.VMEM((groups * piece, length + piece), F32),
                pltpu.VMEM((2, ndp, groups, part), F32),
                pltpu.VMEM((2, ndp, groups, part), F32),
                *[dma((hn,)) for _ in range(6)],
                dma((2,)),
                *[dma((hn,)) for _ in range(4)],
                dma((2, ndp)), dma((2, ndp)),
            ],
            compiler_params=pltpu.CompilerParams(
                collective_id=0, has_side_effects=True, vmem_limit_bytes=40 * 1024 * 1024
            ),
            cost_estimate=pl.CostEstimate(
                flops=3 * channels * length * length // n,
                bytes_accessed=12 * piece * channels,
                transcendentals=0,
            ),
        )(q, k, v, ct, filters)
        conv = conv.reshape(query.shape).astype(F32)
        adjoint = adjoint.reshape(query.shape).astype(F32)
        output = (query.astype(F32) * conv).astype(BF16)
        grad_query = (cotangent.astype(F32) * conv).astype(BF16)
        grad_key = (adjoint * value.astype(F32)).astype(BF16)
        grad_value = (adjoint * key_in.astype(F32)).astype(BF16)
        return output, grad_query, grad_key, grad_value, grad_filter

    signal = P("dp", "ctx", None)
    return jax.shard_map(
        local,
        mesh=mesh,
        in_specs=(signal, signal, signal, signal, P("ctx", None)),
        out_specs=(signal, signal, signal, signal, P("ctx", "dp")),
        check_vma=False,
    )
```

time: 41.3 us -> 34.8 us (0.84)
  Pallas kernels: 34.1 us -> 27.3 us
    pallas_call x1, Pallas kernels: 34.1 us -> 27.3 us  [local(): pl.pallas_call(functools.partial(kernel, n, ndp, scale), out_shape=(jax.S...]
where the time goes in v2:
time: 34.8 us; the launch traced here: 34.2 us
  Pallas kernels  27.3 us (78%)
  local copies, waits for them, and re-layouts  5.08 us (15%)
  other arithmetic  1.22 us (4%)
  between operations  0.65 us (2%)
    pallas_call x1, Pallas kernels, local(): pl.pallas_call(functools.partial(kernel, n, ndp, scale), out_shape=(jax.S...  27.3 us
    unnamed x11, local copies, waits for them, and re-layouts  5.08 us
    convert_element_type x1, other arithmetic, local(): grad_query = (cotangent.astype(F32) * conv).astype(BF16)  1.22 us

profile of v2, /device:TPU:0, one launch (start us, length us, event | category | flops | bytes accessed | tf_op | source)
XLA Modules:
  0.0 34.2 jit_solution(8217189920234402506)
XLA Ops:
  0.6 0.0 copy-start
  0.6 0.9 %copy-done = bf16[1,128,1024]{2,1,0:T(8,128)(2,1)S(1)} copy-done((bf16[1,128,1024]{2,1,0:T(8,128)(2,1)S(1)}, bf16[1,128,1024]{2,1,0:T(8,128)(2,1)}, u32[]{:S(2)}) %copy-start) | copy-done | bytes 262168
  1.6 0.0 copy-start.1
  1.6 0.9 %copy-done.1 = bf16[1,128,1024]{2,1,0:T(8,128)(2,1)S(1)} copy-done((bf16[1,128,1024]{2,1,0:T(8,128)(2,1)S(1)}, bf16[1,128,1024]{2,1,0:T(8,128)(2,1)}, u32[]{:S(2)}) %copy-start.1) | copy-done | bytes 262168
  2.5 0.0 copy-start.2
  2.5 0.9 %copy-done.2 = bf16[1,128,1024]{2,1,0:T(8,128)(2,1)S(1)} copy-done((bf16[1,128,1024]{2,1,0:T(8,128)(2,1)S(1)}, bf16[1,128,1024]{2,1,0:T(8,128)(2,1)}, u32[]{:S(2)}) %copy-start.2) | copy-done | bytes 262168
  3.5 0.0 copy-start.3
  3.5 0.9 %copy-done.3 = bf16[1,128,1024]{2,1,0:T(8,128)(2,1)S(1)} copy-done((bf16[1,128,1024]{2,1,0:T(8,128)(2,1)S(1)}, bf16[1,128,1024]{2,1,0:T(8,128)(2,1)}, u32[]{:S(2)}) %copy-start.3) | copy-done | bytes 262168
  4.4 0.0 copy-start.4
  4.4 0.7 %copy-done.4 = bf16[4,1024]{1,0:T(4,128)(2,1)S(1)} copy-done((bf16[4,1024]{1,0:T(4,128)(2,1)S(1)}, bf16[4,1024]{1,0:T(4,128)(2,1)}, u32[]{:S(2)}) %copy-start.4) | copy-done | bytes 8216
  5.1 27.3 %shard_map.92 = (bf16[128,1024]{1,0:T(8,128)(2,1)S(1)}, bf16[128,1024]{1,0:T(8,128)(2,1)S(1)}, f32[4,256]{1,0:T(4,128)S(1)}) custom-call(bf16[128,1024]{1,0:T(8,128)(2,1)S(1)} %bitcast.13, bf16[128,1024]{1,0:T(8,128)(2,1)S(1)} %bitcast.14, bf16[128,1024]{1,0:T(8,128)(2,1)S(1)} %bitcast.15, bf16[128,1024]{1,0:T(8,128)(2,1)S(1)} %bitcast.12, ...), custom_call_target="tpu_custom_call" | custom-call | flops 402653184 | bytes 1572864 | tf_op jit(solution)/shard_map/pallas_call | solution.py:319
  32.4 1.2 %fusion.1 = (bf16[1,128,1024]{2,1,0:T(8,128)(2,1)}, bf16[1,128,1024]{2,1,0:T(8,128)(2,1)}, bf16[1,128,1024]{2,1,0:T(8,128)(2,1)}, bf16[1,128,1024]{2,1,0:T(8,128)(2,1)}) fusion(bf16[1,128,1024]{2,1,0:T(8,128)(2,1)S(1)} %copy-done, bf16[128,1024]{1,0:T(8,128)(2,1)S(1)} %get-tuple-element.8, bf16[1,128,1024]{2,1,0:T(8,128)(2,1)S(1)} %copy-done.1, ...), kind=kLoop, calls=%fused_computation.5 | loop fusion | flops 1835008 | bytes 2621440 | tf_op jit(solution)/shard_map/convert_element_type | solution.py:363
  33.7 0.6 %copy.11 = f32[4,256]{1,0:T(4,128)} copy(f32[4,256]{1,0:T(4,128)S(1)} %get-tuple-element.26) | data formatting | bytes 8192
Async XLA Ops:
  0.6 1.0 %copy-start = (bf16[1,128,1024]{2,1,0:T(8,128)(2,1)S(1)}, bf16[1,128,1024]{2,1,0:T(8,128)(2,1)}, u32[]{:S(2)}) copy-start(bf16[1,128,1024]{2,1,0:T(8,128)(2,1)} %param.8) | copy-start | bytes 786436
  1.6 0.9 %copy-start.1 = (bf16[1,128,1024]{2,1,0:T(8,128)(2,1)S(1)}, bf16[1,128,1024]{2,1,0:T(8,128)(2,1)}, u32[]{:S(2)}) copy-start(bf16[1,128,1024]{2,1,0:T(8,128)(2,1)} %param.5) | copy-start | bytes 786436
  2.5 0.9 %copy-start.2 = (bf16[1,128,1024]{2,1,0:T(8,128)(2,1)S(1)}, bf16[1,128,1024]{2,1,0:T(8,128)(2,1)}, u32[]{:S(2)}) copy-start(bf16[1,128,1024]{2,1,0:T(8,128)(2,1)} %param.6) | copy-start | bytes 786436
  3.5 0.9 %copy-start.3 = (bf16[1,128,1024]{2,1,0:T(8,128)(2,1)S(1)}, bf16[1,128,1024]{2,1,0:T(8,128)(2,1)}, u32[]{:S(2)}) copy-start(bf16[1,128,1024]{2,1,0:T(8,128)(2,1)} %param.7) | copy-start | bytes 786436
  4.4 0.7 %copy-start.4 = (bf16[4,1024]{1,0:T(4,128)(2,1)S(1)}, bf16[4,1024]{1,0:T(4,128)(2,1)}, u32[]{:S(2)}) copy-start(bf16[4,1024]{1,0:T(4,128)(2,1)} %f_hbm.1) | copy-start | bytes 24580

commit v3 on v2

--- a/solution.py
+++ b/solution.py
@@ -9,6 +9,7 @@
 from jax.sharding import PartitionSpec as P
 
 CPG = 32
+STEPS = 2
 MESH = pl.DeviceIdType.MESH
 F32 = jnp.float32
 BF16 = jnp.bfloat16
@@ -23,7 +24,7 @@
     q_hbm, k_hbm, v_hbm, ct_hbm, f_hbm,
     conv_ref, adj_ref, gf_ref,
     q_ref, k_ref, v_ref, ct_ref, f_ref, load_sem,
-    slong, sshort, rlong, rshort, rcross, fpair, strips, mlong, mshort,
+    slong, sshort, rlong, rshort, rcross, fpair, strips, crossed, mlong, mshort,
     tlong, tshort, backl, backs, lhs, rhs, lags, gsend, grecv,
     slong_sem, sshort_sem, scross_sem, rlong_sem, rshort_sem, rcross_sem, f_sem,
     tlong_sem, tshort_sem, backl_sem, backs_sem, gsend_sem, grecv_sem,
@@ -70,21 +71,31 @@
     at_col = lax.broadcasted_iota(jnp.int32, (piece, piece), 1)
     flip = jnp.where(at_row + at_col == piece - 1, 1.0, 0.0).astype(BF16)
 
-    loads[0].wait()
-    loads[1].wait()
-    mixed = (k_ref[...].astype(F32) * v_ref[...].astype(F32)).astype(BF16)
-    turned = dot(flip, mixed).astype(BF16)
-    loads[2].wait()
-    loads[3].wait()
-    gradin = (ct_ref[...].astype(F32) * q_ref[...].astype(F32)).astype(BF16)
-    long = choose(gradin, turned)
-    short = choose(turned, gradin)
-    for owner in range(hn):
-        for block in range(2):
-            to = slice(block * width, (block + 1) * width)
-            at = (owner + block * hn) * width
-            slong[owner, :, to] = long[:, at : at + width]
-            sshort[owner, :, to] = short[:, at : at + width]
+    def gate_mixed(staged):
+        loads[0].wait()
+        loads[1].wait()
+        mixed = (k_ref[...].astype(F32) * v_ref[...].astype(F32)).astype(BF16)
+        stage(staged, dot(flip, mixed).astype(BF16))
+
+    def gate_gradin(staged):
+        loads[2].wait()
+        loads[3].wait()
+        stage(staged, (ct_ref[...].astype(F32) * q_ref[...].astype(F32)).astype(BF16))
+
+    def stage(staged, values):
+        for owner in range(hn):
+            for block in range(2):
+                at = (owner + block * hn) * width
+                staged[owner, :, block * width : (block + 1) * width] = values[:, at : at + width]
+
+    @pl.when(half == 0)
+    def _():
+        gate_mixed(sshort)
+
+    @pl.when(half != 0)
+    def _():
+        gate_gradin(sshort)
+
     loads[4].wait()
     fpair[half] = f_ref[...].astype(F32)
     pl.semaphore_wait(barrier, n - 1 + 2 * (ndp - 1))
@@ -110,16 +121,28 @@
             sshort.at[owner], rcross.at[short_slot], scross_sem.at[owner],
             rcross_sem.at[short_slot], (1 - half) * hn + owner,
         ))
+    for each in outward:
+        each.start()
+    rshort[short_slot] = sshort[rank]
+
+    @pl.when(half == 0)
+    def _():
+        gate_gradin(slong)
+
+    @pl.when(half != 0)
+    def _():
+        gate_mixed(slong)
+
+    later = []
     for step in range(1, hn):
         owner = lax.rem(rank + step, hn)
-        outward.append(copy(
+        later.append(copy(
             slong.at[owner], rlong.at[long_slot], slong_sem.at[owner],
             rlong_sem.at[long_slot], half * hn + owner,
         ))
-    for each in outward:
+    for each in later:
         each.start()
     rlong[long_slot] = slong[rank]
-    rshort[short_slot] = sshort[rank]
 
     copy(
         fpair.at[1 - half], fpair.at[1 - half], f_sem.at[0], f_sem.at[1], partner
@@ -146,19 +169,18 @@
                 landed[slot, :, side : side + width] * picks[g % groups]
             )
 
-    def convolve(masked, depth, staged, landed, out_sem, in_sem, own_slot, mirrored):
+    def convolve(masked, beyond, staged, landed, out_sem, in_sem, own_slot, mirrored):
         for pair in range(hn // 2):
             first = 2 * pair * piece
             for block in range(2):
-                total = None
+                span = slice(block * width, (block + 1) * width)
+                total = None if beyond is None else beyond[first : first + 2 * piece, span]
                 for g in range(block * groups, (block + 1) * groups):
-                    term = dot(strips[g, :, : depth - first], masked[g, first:, :])
+                    term = dot(strips[g, :, : reach - first], masked[g, first:reach, :])
                     total = term if total is None else total + term
                 total = total.astype(BF16)
                 for at in range(2):
-                    staged[2 * pair + at, :, block * width : (block + 1) * width] = total[
-                        at * piece : (at + 1) * piece
-                    ]
+                    staged[2 * pair + at, :, span] = total[at * piece : (at + 1) * piece]
             for at in range(2):
                 slot = 2 * pair + at
                 source = mirrored * (hn - 1 - slot) + (1 - mirrored) * slot
@@ -179,17 +201,25 @@
         def _():
             arrive(rshort, rshort_sem, slot)
         spread_out(rshort, slot, mshort, slot)
-    convolve(mshort, reach, tshort, backs, tshort_sem, backs_sem, short_slot, 1 - half)
+    convolve(mshort, None, tshort, backs, tshort_sem, backs_sem, short_slot, 1 - half)
 
     for slot in range(hn):
         arrive(rcross, rcross_sem, slot)
         spread_out(rcross, slot, mlong, hn + slot)
+    for pair in range(hn // 2):
+        first = 2 * pair * piece
+        for block in range(2):
+            total = None
+            for g in range(block * groups, (block + 1) * groups):
+                term = dot(strips[g, :, reach - first : length - first], mlong[g, reach:, :])
+                total = term if total is None else total + term
+            crossed[first : first + 2 * piece, block * width : (block + 1) * width] = total
     for slot in range(hn):
         @pl.when(slot != long_slot)
         def _():
             arrive(rlong, rlong_sem, slot)
         spread_out(rlong, slot, mlong, slot)
-    convolve(mlong, 2 * reach, tlong, backl, tlong_sem, backl_sem, long_slot, half)
+    convolve(mlong, crossed, tlong, backl, tlong_sem, backl_sem, long_slot, half)
 
     def lanes(values, role):
         left, right = values[:, :width], values[:, width:]
@@ -288,7 +318,7 @@
     gf_ref[...] = gathered
 
     filters_copy.wait_send()
-    for each in outward:
+    for each in outward + later:
         each.wait_send()
     for slot in range(hn):
         @pl.when(slot != short_slot)
@@ -302,6 +332,15 @@
             copy(
                 tlong.at[slot], backl.at[rank], tlong_sem.at[slot], backl_sem.at[rank], partner
             ).wait_send()
+
+
+def finish(q, k, v, ct, conv, adjoint, gf, output, grad_q, grad_k, grad_v, grad_f):
+    conv_wide, adjoint_wide = conv[...].astype(F32), adjoint[...].astype(F32)
+    output[...] = (q[...].astype(F32) * conv_wide).astype(BF16)
+    grad_q[...] = (ct[...].astype(F32) * conv_wide).astype(BF16)
+    grad_k[...] = (adjoint_wide * v[...].astype(F32)).astype(BF16)
+    grad_v[...] = (adjoint_wide * k[...].astype(F32)).astype(BF16)
+    grad_f[...] = gf[...]
 
 
 def solution(mesh):
@@ -335,6 +374,7 @@
                 *[pltpu.VMEM((hn, piece, 2 * width), BF16) for _ in range(5)],
                 pltpu.VMEM((2, groups, length), F32),
                 pltpu.VMEM((2 * groups, 2 * piece, length), BF16),
+                pltpu.VMEM((hn * piece, 2 * width), F32),
                 pltpu.VMEM((2 * groups, length, width), BF16),
                 pltpu.VMEM((2 * groups, length // 2, width), BF16),
                 *[pltpu.VMEM((hn, piece, 2 * width), BF16) for _ in range(4)],
@@ -349,7 +389,7 @@
                 dma((2, ndp)), dma((2, ndp)),
             ],
             compiler_params=pltpu.CompilerParams(
-                collective_id=0, has_side_effects=True, vmem_limit_bytes=40 * 1024 * 1024
+                collective_id=0, has_side_effects=True, vmem_limit_bytes=62 * 1024 * 1024
             ),
             cost_estimate=pl.CostEstimate(
                 flops=3 * channels * length * length // n,
@@ -357,12 +397,19 @@
                 transcendentals=0,
             ),
         )(q, k, v, ct, filters)
-        conv = conv.reshape(query.shape).astype(F32)
-        adjoint = adjoint.reshape(query.shape).astype(F32)
-        output = (query.astype(F32) * conv).astype(BF16)
-        grad_query = (cotangent.astype(F32) * conv).astype(BF16)
-        grad_key = (adjoint * value.astype(F32)).astype(BF16)
-        grad_value = (adjoint * key_in.astype(F32)).astype(BF16)
+        steps = STEPS if piece % (16 * STEPS) == 0 else 1
+        rows = pl.BlockSpec((piece // steps, channels), lambda at: (at, 0))
+        terms = pl.BlockSpec((groups, part), lambda at: (0, 0))
+        gated = jax.ShapeDtypeStruct((piece, channels), BF16)
+        *gated, grad_filter = pl.pallas_call(
+            finish,
+            grid=(steps,),
+            out_shape=(gated, gated, gated, gated, jax.ShapeDtypeStruct((groups, part), F32)),
+            in_specs=[rows] * 6 + [terms],
+            out_specs=(rows, rows, rows, rows, terms),
+            compiler_params=pltpu.CompilerParams(vmem_limit_bytes=62 * 1024 * 1024),
+        )(q, k, v, ct, conv, adjoint, grad_filter)
+        output, grad_query, grad_key, grad_value = (x.reshape(query.shape) for x in gated)
         return output, grad_query, grad_key, grad_value, grad_filter
 
     signal = P("dp", "ctx", None)

time: 34.8 us -> 31.6 us (0.908)
  local copies, waits for them, and re-layouts: 5.08 us -> 0 us
  Pallas kernels: 27.3 us -> 30.4 us
  other arithmetic: 1.22 us -> 0 us
    unnamed x11 -> x0, local copies, waits for them, and re-layouts: 5.08 us -> none
    pallas_call x0 -> x1, Pallas kernels: none -> 2.31 us  [local(): pl.pallas_call(finish, grid=(steps,), out_shape=(gated, gated, gated, gat...]
    convert_element_type x1 -> x0, other arithmetic: 1.22 us -> none  [local(): grad_query = (cotangent.astype(F32) * conv).astype(BF16)]
    pallas_call x1, Pallas kernels: 27.3 us -> 28.1 us  [local(): pl.pallas_call(functools.partial(kernel, n, ndp, scale), out_shape=(jax.S...]
where the time goes in v3:
time: 31.6 us; the launch traced here: 31.1 us
  Pallas kernels  30.4 us (96%)
  between operations  0.64 us (2%)
    pallas_call x1, Pallas kernels, local(): pl.pallas_call(functools.partial(kernel, n, ndp, scale), out_shape=(jax.S...  28.1 us
    pallas_call x1, Pallas kernels, local(): pl.pallas_call(finish, grid=(steps,), out_shape=(gated, gated, gated, gat...  2.31 us

profile of v3, /device:TPU:0, one launch (start us, length us, event | category | flops | bytes accessed | tf_op | source)
XLA Modules:
  0.0 31.1 jit_solution(7703937231634180242)
XLA Ops:
  0.6 28.1 %shard_map.92 = (bf16[128,1024]{1,0:T(8,128)(2,1)}, bf16[128,1024]{1,0:T(8,128)(2,1)}, f32[4,256]{1,0:T(4,128)}) custom-call(bf16[128,1024]{1,0:T(8,128)(2,1)} %bitcast.8, bf16[128,1024]{1,0:T(8,128)(2,1)} %bitcast.10, bf16[128,1024]{1,0:T(8,128)(2,1)} %bitcast.12, bf16[128,1024]{1,0:T(8,128)(2,1)} %bitcast.14, bf16[4,1024]{1,0:T(4,128)(2,1)} %f_hbm.1), custom_call_target="tpu_custom_call" | custom-call | flops 402653184 | bytes 1572864 | tf_op jit(solution)/shard_map/pallas_call | solution.py:358
  28.7 2.3 %shard_map.93 = (bf16[128,1024]{1,0:T(8,128)(2,1)}, bf16[128,1024]{1,0:T(8,128)(2,1)}, bf16[128,1024]{1,0:T(8,128)(2,1)}, bf16[128,1024]{1,0:T(8,128)(2,1)}, f32[4,256]{1,0:T(4,128)}) custom-call(bf16[128,1024]{1,0:T(8,128)(2,1)} %bitcast.9, bf16[128,1024]{1,0:T(8,128)(2,1)} %bitcast.11, bf16[128,1024]{1,0:T(8,128)(2,1)} %bitcast.13, ...), custom_call_target="tpu_custom_call" | custom-call | tf_op jit(solution)/shard_map/pallas_call | solution.py:404
